TPU v7x, 256 devices: a whole 4x4x8 slice. The times are simulated.
256 devices in a mesh: fr: 2 (over y_lo), gr: 16 (over z, core), gc: 8 (over y_hi, x).
Axes of the slice: x: 4, y: 4 (y_hi: 2, y_lo: 2; y = y_hi * 2 + y_lo), z: 8, core: 2. Of those that a mesh axis runs over, the one named last changes fastest.
Arguments:
- front: bfloat16 [6, 8192, 8192], P('fr', 'gr', 'gc'), parts along dimension 0
- omega: bfloat16 [6, 8192, 256], P('fr', 'gc'), parts along dimension 0, may hold values from -6 to 6
- child_sketch: bfloat16 [6, 2, 2048, 256], P('fr', None, ('gr', 'gc')), parts along dimension 0, may hold values from -6 to 6
- child_map: int32 [6, 2, 2048], P('fr', None, ('gr', 'gc')), parts along dimension 0, may hold values from 0 to 8191, as said below
- picks: int32 [6, 16, 128], P('fr'), parts along dimension 0, may hold values from 0 to 511, as said below
Outputs:
- sketch: float32 [6, 8192, 256], P('fr', 'gr', 'gc'), parts along dimension 0
- basis: float32 [6, 8192, 128], P('fr', 'gr'), parts along dimension 0
- coupling: bfloat16 [6, 2048, 2048], P('fr', 'gr', 'gc'), parts along dimension 0
There are 2 independent parts, one for each index of `fr`. A program takes and returns all parts, laid end to end along the dimension named above; each array names one. Nothing has to cross between parts.
Inputs may be any that keep to these rules, and one draw needn't show every extreme that they name: `child_map`: within each child the 2048 entries are distinct. Within each block the 128 picks are distinct.
All inputs are finite; a program needn't handle non-finite values.
Results may differ from a plain program's by a relative error of at most 0.0004.
Values may be sent and summed in bfloat16 or wider, within the bound.
A program may use at most 64 MiB of HBM per device.

v0:
```python
import functools
import math

import jax
import jax.numpy as jnp
from jax import lax
from jax.experimental import pallas as pl
from jax.experimental.pallas import tpu as pltpu
from jax.sharding import PartitionSpec as P

MESH = pl.DeviceIdType.MESH
F32 = jnp.float32
BF16 = jnp.bfloat16
I32 = jnp.int32
NF = 3
LB = 512
R = 256
K = 128
NC = 8
NZ = 8
CH = LB // NC
MSG = CH + 1
SLOT = CH + 8
STEP = math.log(2.0) / 8.0
TOP = 32760.0
SMALLEST = 2.0**-110
NEAR = 3e-3
OTHER_CORE = (4, -3, 3, -2, 2, -1, 1)
PEERS = ((1, 2), (1, 1), (1, 3), (1, 0), (0, 2), (0, 1), (0, 3))


def thresholds(count):
    low, table = 1.0 - NEAR, []
    for _ in range(count):
        table.append(low)
        gain = low / (2.0 - low)
        low = gain / (1.0 + math.sqrt(1.0 - gain))
    return table


def dot(a, b):
    return lax.dot_general(a, b, (((1,), (0,)), ((), ())), preferred_element_type=F32)


def dot_t(a, b):
    return lax.dot_general(a, b, (((1,), (1,)), ((), ())), preferred_element_type=F32)


def split(x):
    hi = x.astype(BF16)
    return hi, (x - hi.astype(F32)).astype(BF16)


def diagonal(rows, columns):
    shape = (rows, columns)
    return lax.broadcasted_iota(I32, shape, 0) == lax.broadcasted_iota(I32, shape, 1)


def encode(x):
    top = jnp.maximum(jnp.max(jnp.abs(x), axis=1, keepdims=True), SMALLEST)
    level = jnp.ceil(jnp.log(top) * (1.0 / STEP))
    q = jnp.round(x * (jnp.exp(level * -STEP) * TOP)).astype(I32)
    packed = (q[:, : R // 2] << 16) | (q[:, R // 2 :] & 0xFFFF)
    levels = jnp.sum(jnp.where(diagonal(CH, 128), level, 0.0), axis=0, keepdims=True)
    return packed, levels.astype(I32)


def decode(packed, levels):
    level = jnp.sum(jnp.where(diagonal(CH, 128), levels.astype(F32), 0.0), axis=1, keepdims=True)
    scale = jnp.exp(level * STEP) * (1.0 / TOP)
    first = (packed >> 16).astype(F32) * scale
    second = ((packed << 16) >> 16).astype(F32) * scale
    return first, second


def exchange_kernel(
    front_hbm, omega_hbm, child_hbm, map_hbm, picks_hbm,
    gram_ref, cross_ref, own_ref, energy_ref, coupling_ref,
    front, omega, child_all, maps, map_in, picks_ref, partial, rs_out, rs_in, ag_in, en1, en2, pick_rows, high_part, low_part, own_half,
    load_sem, child_s, child_r, map_s, map_r, core_s, core_r, rs_s, rs_r, ag_s, ag_r, e1_s, e1_r, e2_s, e2_r,
):
    fr = lax.axis_index("fr")
    gr = lax.axis_index("gr")
    gc = lax.axis_index("gc")
    z = gr // 2
    core = gr % 2

    def z_peer(d):
        zz = lax.rem(z + d + NZ, NZ)
        return zz, (fr, zz * 2 + core, gc)

    def c_peer(d):
        up, right = d
        cc = lax.rem(gc // 4 + up, 2) * 4 + lax.rem(gc % 4 + right + core * 2 * (right % 2), 4)
        return cc, (fr, gr, cc)

    def g_peer(d):
        gg = lax.rem(gr + d + 16, 16)
        return gg, (fr, gg, gc)

    partner = (fr, z * 2 + (1 - core), gc)

    loads = []
    own_child = []
    for f in range(NF):
        own_child.append(pltpu.make_async_copy(child_hbm.at[f], child_all.at[f, core, z], load_sem.at[f]))
        own_child[f].start()
    own_map = pltpu.make_async_copy(map_hbm, map_in, load_sem.at[9])
    own_map.start()
    for f in range(NF):
        a = pltpu.make_async_copy(front_hbm.at[f], front.at[f], load_sem.at[3 + f])
        b = pltpu.make_async_copy(omega_hbm.at[f], omega.at[f], load_sem.at[6 + f])
        b.start()
        a.start()
        loads.append((a, b))

    picks_load = pltpu.make_async_copy(picks_hbm, picks_ref, load_sem.at[10])
    picks_load.start()

    barrier = pltpu.get_barrier_semaphore()
    for d in range(1, 16):
        pl.semaphore_signal(barrier, inc=1, device_id=g_peer(d)[1], device_id_type=MESH)
    for d in PEERS:
        pl.semaphore_signal(barrier, inc=1, device_id=c_peer(d)[1], device_id_type=MESH)
    own_map.wait()
    lane = lax.broadcasted_iota(I32, (1, 128), 1)
    tile = []
    for f in range(NF):
        both = jnp.concatenate([map_in[f, 0:1, :], map_in[f, 1:2, :]] * 4, axis=1)
        tile.append(jnp.where(lane // 32 == z % 4, both, 0))
    maps[core, z] = jnp.concatenate(tile + [jnp.zeros((8 - NF, 128), I32)], axis=0)
    pl.semaphore_wait(barrier, 22)

    sends = []

    def send(src, dst, s, r, device):
        copy = pltpu.make_async_remote_copy(
            src_ref=src, dst_ref=dst, send_sem=s, recv_sem=r, device_id=device, device_id_type=MESH
        )
        copy.start()
        sends.append(copy)

    def arrive(dst, s, r, device):
        pltpu.make_async_remote_copy(
            src_ref=dst, dst_ref=dst, send_sem=s, recv_sem=r, device_id=device, device_id_type=MESH
        ).wait_recv()

    for d in (4, 3, 5, 2, 6, 1, 7):
        device = z_peer(d)[1]
        send(maps.at[core, z, 0:NF, :], maps.at[core, z, 0:NF, :], map_s.at[d - 1], map_r.at[z], device)

    def send_rows(f, origin, to, slot):
        ref = child_all.at[f, core, origin]
        send(ref, ref, child_s.at[f, slot], child_r.at[f, origin], z_peer(to)[1])

    def rows_arrive(f, origin, slot):
        arrive(child_all.at[f, core, origin], child_s.at[f, slot], child_r.at[f, origin], z_peer(1)[1])

    direct = (4, 3, -3, 2, -2, 1, -1)
    def send_children(f):
        own_child[f].wait()
        for slot, pair in enumerate(zip(direct, OTHER_CORE)):
            send_rows(f, z, jnp.where(core == 0, *pair), slot)

    send_children(0)
    send_children(1)
    send_children(2)

    for f in range(NF):
        loads[f][0].wait()
        loads[f][1].wait()
        for half in range(2):
            rows = pl.ds(half * LB, LB)
            off = gr != 2 * gc + half
            omega[f, rows, :] = jnp.where(off, omega[f, rows, :], jnp.zeros((), BF16))
        for r in range(4):
            rows = pl.ds(r * 128, 128)
            partial[f, rows, :] = dot(front[f, rows, :], omega[f])

    picks_load.wait()
    for f in range(NF):
        picked = picks_ref[f, pl.ds(gr, 1), :]
        down = jnp.transpose(jnp.broadcast_to(picked, (K, K)))
        lanes = lax.broadcasted_iota(I32, (K, K), 1)
        pick_rows[f] = jnp.concatenate([(down == lanes + 128 * t).astype(BF16) for t in range(4)], axis=1)
        mine = dot(pick_rows[f], front[f]).astype(BF16)
        for half in range(2):
            wanted = picks_ref[f, pl.ds(2 * gc + half, 1), :]
            pick_columns = (lax.broadcasted_iota(I32, (LB, K), 0) == wanted).astype(BF16)
            coupling_ref[f, :, half * K : (half + 1) * K] = dot(
                mine[:, half * LB : (half + 1) * LB], pick_columns
            ).astype(BF16)

    for d in range(1, NZ):
        zz, device = z_peer(-d)
        arrive(maps.at[core, zz, 0:NF, :], map_s.at[d - 1], map_r.at[zz], device)
    send(maps.at[core], maps.at[core], map_s.at[7], map_r.at[8], partner)

    targets = None
    for f in range(NF):
        for d in direct:
            rows_arrive(f, z_peer(d)[0], 0)
        send(child_all.at[f, core], child_all.at[f, core], core_s.at[f], core_r.at[f], partner)

        if targets is None:
            arrive(maps.at[1 - core], map_s.at[7], map_r.at[8], partner)
            targets = []
            for k in range(2):
                for h in range(2):
                    tile = maps[k, 4 * h]
                    for t in range(1, 4):
                        tile = tile + maps[k, 4 * h + t]
                    targets.append(tile - gr * LB)
        arrive(child_all.at[f, 1 - core], core_s.at[f], core_r.at[f], partner)

        rows = lax.broadcasted_iota(I32, (LB, 128), 0)
        hits = jnp.concatenate([(rows == tile[f : f + 1, :]).astype(BF16) for tile in targets], axis=1)
        whole = partial[f] + dot(hits, child_all[f].reshape(2 * NZ * 32, R))
        partial[f] = whole
        for c in range(NC):
            packed, levels = encode(whole[c * CH : (c + 1) * CH])
            rs_out[f, c, 0:CH, :] = packed
            rs_out[f, c, CH:MSG, :] = levels
        for slot, d in enumerate(PEERS):
            cc, device = c_peer(d)
            send(rs_out.at[f, cc, 0:MSG, :], rs_in.at[f, gc, 0:MSG, :], rs_s.at[f, slot], rs_r.at[f, gc], device)

    energies = []
    for f in range(NF):
        own = partial[f, pl.ds(gc * CH, CH), :]
        first, second = own[:, :128], own[:, 128:]
        for d in PEERS:
            cc, device = c_peer(d)
            arrive(rs_in.at[f, cc, 0:MSG, :], rs_s.at[f, 0], rs_r.at[f, cc], device)
        for d in PEERS:
            cc = c_peer(d)[0]
            a, b = decode(rs_in[f, cc, 0:CH, :], rs_in[f, cc, CH : CH + 1, :])
            first, second = first + a, second + b
        total = jnp.concatenate([first, second], axis=1)
        packed, levels = encode(total)
        ag_in[f, gc, 0:CH, :] = packed
        ag_in[f, gc, CH:MSG, :] = levels
        energies.append(jnp.sum(first * first + second * second, axis=0, keepdims=True))
        if f == NF - 1:
            en1[gr] = jnp.concatenate(energies + [jnp.zeros((8 - NF, 128), F32)], axis=0)
            for d in range(1, 16):
                send(en1.at[gr], en1.at[gr], e1_s.at[d - 1], e1_r.at[gr], g_peer(d)[1])
        for slot, d in enumerate(PEERS):
            cc, device = c_peer(d)
            send(ag_in.at[f, gc, 0:MSG, :], ag_in.at[f, gc, 0:MSG, :], ag_s.at[f, slot], ag_r.at[f, gc], device)

    for d in range(1, 16):
        gg, device = g_peer(-d)
        arrive(en1.at[gg], e1_s.at[d - 1], e1_r.at[gg], device)
    en2[gc] = functools.reduce(lambda a, b: a + b, [en1[g] for g in range(16)])
    for slot, d in enumerate(PEERS):
        send(en2.at[gc], en2.at[gc], e2_s.at[slot], e2_r.at[gc], c_peer(d)[1])

    for f in range(NF):
        if f == NF - 1:
            for copy in sends:
                copy.wait_send()
        for d in PEERS:
            cc, device = c_peer(d)
            arrive(ag_in.at[f, cc, 0:MSG, :], ag_s.at[f, 0], ag_r.at[f, cc], device)
        for c in range(NC):
            rows = slice(c * CH, (c + 1) * CH)
            a, b = decode(ag_in[f, c, 0:CH, :], ag_in[f, c, CH : CH + 1, :])
            own_half[rows, :] = jnp.where(gc < 4, a, b)
            a0, a1 = split(a)
            b0, b1 = split(b)
            high_part[rows, 0:128] = a0
            high_part[rows, 128:256] = b0
            low_part[rows, 0:128] = a1
            low_part[rows, 128:256] = b1
        s0, s1 = high_part[...], low_part[...]
        k0 = dot(pick_rows[f], s0).astype(BF16)
        k1 = dot(pick_rows[f], s1).astype(BF16)
        parts = jnp.concatenate([k0, k1], axis=0)
        gram = dot_t(k0, parts)
        gram_ref[f] = gram[:, :K] + (gram[:, K:] + dot_t(k1, k0))
        cross = dot_t(s0, parts)
        cross_ref[f] = cross[:, :K] + (cross[:, K:] + dot_t(s1, k0))
        half_t = jnp.transpose(own_half[...])
        quarter = lax.rem(gc, 4)
        own = half_t[0:32]
        for t in range(1, 4):
            own = jnp.where(quarter == t, half_t[32 * t : 32 * t + 32], own)
        own_ref[f] = own

    for d in PEERS:
        cc, device = c_peer(d)
        arrive(en2.at[cc], e2_s.at[0], e2_r.at[cc], device)
    energy_ref[...] = functools.reduce(lambda a, b: a + b, [en2[c] for c in range(NC)])


def mm3(a, b):
    left = jnp.concatenate(split(a), axis=1)
    right = jnp.concatenate(split(b), axis=1)
    both = dot(left, jnp.concatenate([right, right], axis=0))
    return both[:, :K] + both[:, K:]


def high(a, b):
    return lax.dot_general(
        a, b, (((1,), (0,)), ((), ())), preferred_element_type=F32, precision=lax.Precision.HIGHEST
    )


def solve_kernel(
    gram_ref, cross_ref, own_ref, energy_ref, coupling_ref,
    own_hbm, basis_hbm, coupling_hbm,
    shifted, state, lows, basis, sem,
):
    stores = [
        pltpu.make_async_copy(coupling_ref, coupling_hbm, sem.at[0]),
        pltpu.make_async_copy(own_ref, own_hbm, sem.at[1]),
    ]
    for store in stores:
        store.start()
    eye = diagonal(K, K)
    steps = jnp.zeros((1, 1), F32)
    for f in range(NF):
        energy = jnp.sum(energy_ref[f : f + 1, :], axis=1, keepdims=True)
        level = 0.5 * energy / 8192.0 + 1e-05
        gram = gram_ref[f] + jnp.where(eye, level, 0.0)
        bound = jnp.max(jnp.sum(jnp.abs(gram), axis=0, keepdims=True), axis=1, keepdims=True)
        trace = jnp.sum(
            jnp.sum(jnp.where(eye, gram, 0.0), axis=0, keepdims=True), axis=1, keepdims=True
        )
        top = jnp.minimum(bound, trace)
        c = 2.0 / (level + top)
        low = level * c
        gain = low * (2.0 - low)
        s = 2.0 / (1.0 + gain)
        state[f] = jnp.where(eye, 2.0 * s * c, 0.0) - (s * c * c) * gram
        shifted[f] = gram
        low = s * gain
        lows[f : f + 1, :] = jnp.broadcast_to(low, (1, K))
        needed = jnp.zeros((1, 1), F32)
        for mark in thresholds(14):
            needed = needed + jnp.where(low < mark, 1.0, 0.0)
        steps = jnp.maximum(steps, needed)

    def improve(mm):
        for f in range(NF):
            x = state[f]
            low = lows[f : f + 1, :]
            gain = low * (2.0 - low)
            s = 2.0 / (1.0 + gain)
            lows[f : f + 1, :] = s * gain
            y = (jnp.where(eye, 2.0, 0.0) - mm(shifted[f], x)) * s
            state[f] = mm(x, y)

    count = steps[0, 0].astype(I32)

    @pl.loop(0, count)
    def _(step):
        improve(mm3)

    improve(high)
    for f in range(NF):
        basis[f] = mm3(cross_ref[f], state[f])
        stores.append(pltpu.make_async_copy(basis.at[f], basis_hbm.at[f], sem.at[2 + f]))
        stores[2 + f].start()
    for store in stores:
        store.wait()


def body(front, omega, child_sketch, child_map, picks):
    child = child_sketch.reshape(NF, 32, R)
    any_space = pl.BlockSpec(memory_space=pltpu.HBM)
    vmem = pl.BlockSpec(memory_space=pltpu.VMEM)
    dma = pltpu.SemaphoreType.DMA
    exchanged = pl.pallas_call(
        exchange_kernel,
        out_shape=(
            jax.ShapeDtypeStruct((NF, K, K), F32),
            jax.ShapeDtypeStruct((NF, LB, K), F32),
            jax.ShapeDtypeStruct((NF, 32, LB), F32),
            jax.ShapeDtypeStruct((8, 128), F32),
            jax.ShapeDtypeStruct((NF, K, 2 * K), BF16),
        ),
        in_specs=[any_space] * 5,
        out_specs=(vmem,) * 5,
        scratch_shapes=[
            pltpu.VMEM((NF, LB, 1024), BF16),
            pltpu.VMEM((NF, 1024, R), BF16),
            pltpu.VMEM((NF, 2, NZ, 32, R), BF16),
            pltpu.VMEM((2, NZ, 8, 128), I32),
            pltpu.VMEM((NF, 2, 16), I32),
            pltpu.VMEM((NF, 16, K), I32),
            pltpu.VMEM((NF, LB, R), F32),
            pltpu.VMEM((NF, NC, SLOT, 128), I32),
            pltpu.VMEM((NF, NC, SLOT, 128), I32),
            pltpu.VMEM((NF, NC, SLOT, 128), I32),
            pltpu.VMEM((16, 8, 128), F32),
            pltpu.VMEM((NC, 8, 128), F32),
            pltpu.VMEM((NF, K, LB), BF16),
            pltpu.VMEM((LB, R), BF16),
            pltpu.VMEM((LB, R), BF16),
            pltpu.VMEM((LB, 128), F32),
            dma((11,)),
            dma((NF, 7)), dma((NF, NZ)),
            dma((8,)), dma((9,)),
            dma((NF,)), dma((NF,)),
            dma((NF, 7)), dma((NF, NC)),
            dma((NF, 7)), dma((NF, NC)),
            dma((15,)), dma((16,)),
            dma((7,)), dma((NC,)),
        ],
        compiler_params=pltpu.CompilerParams(
            collective_id=0, has_side_effects=True, vmem_limit_bytes=48 * 2**20
        ),
        name="exchange",
    )(*(pltpu.with_memory_space_constraint(x, pltpu.HBM) for x in (front, omega, child, child_map, picks)))
    own, basis, coupling = pl.pallas_call(
        solve_kernel,
        out_shape=(
            jax.ShapeDtypeStruct((NF, 32, LB), F32),
            jax.ShapeDtypeStruct((NF, LB, K), F32),
            jax.ShapeDtypeStruct((NF, K, 2 * K), BF16),
        ),
        in_specs=[vmem] * 5,
        out_specs=(any_space,) * 3,
        scratch_shapes=[
            pltpu.VMEM((NF, K, K), F32),
            pltpu.VMEM((NF, K, K), F32),
            pltpu.VMEM((8, K), F32),
            pltpu.VMEM((NF, LB, K), F32),
            dma((5,)),
        ],
        compiler_params=pltpu.CompilerParams(vmem_limit_bytes=48 * 2**20),
        name="solve",
    )(*exchanged)
    return jnp.transpose(own, (0, 2, 1)), basis, coupling


def solution(mesh):
    return jax.shard_map(
        body,
        mesh=mesh,
        in_specs=(
            P("fr", "gr", "gc"),
            P("fr", "gc", None),
            P("fr", None, ("gr", "gc"), None),
            P("fr", None, ("gr", "gc")),
            P("fr", None, None),
        ),
        out_specs=(P("fr", "gr", "gc"), P("fr", "gr", None), P("fr", "gr", "gc")),
        check_vma=False,
    )
```

profile of v0, /device:TPU:1, one launch (start us, length us, event | category | flops | bytes accessed | tf_op | source)
XLA Modules:
  0.0 44.5 jit_solution(9493245862463931500)
XLA Ops:
  0.6 41.4 %exchange.1 = (f32[3,128,128]{2,1,0:T(8,128)S(1)}, f32[3,512,128]{2,1,0:T(8,128)S(1)}, f32[3,32,512]{2,1,0:T(8,128)S(1)}, f32[8,128]{1,0:T(8,128)S(1)}, bf16[3,128,256]{2,1,0:T(8,128)(2,1)S(1)}) custom-call(bf16[3,512,1024]{2,1,0:T(8,128)(2,1)} %front_hbm.1, bf16[3,1024,256]{2,1,0:T(8,128)(2,1)} %omega_hbm.1, bf16[3,32,256]{2,1,0:T(8,128)(2,1)} %bitcast.2, ...), custom_call_target="tpu_custom_call" | custom-call | tf_op jit(solution)/shard_map/exchange/pallas_call | solution.py:375
  42.1 2.5 %solve.1 = (f32[3,32,512]{2,1,0:T(8,128)}, f32[3,512,128]{2,1,0:T(8,128)}, bf16[3,128,256]{2,1,0:T(8,128)(2,1)}) custom-call(f32[3,128,128]{2,1,0:T(8,128)S(1)} %get-tuple-element.11.gram_ref, f32[3,512,128]{2,1,0:T(8,128)S(1)} %get-tuple-element.12.cross_ref, f32[3,32,512]{2,1,0:T(8,128)S(1)} %get-tuple-element.13.own_ref, ...), custom_call_target="tpu_custom_call" | custom-call | tf_op jit(solution)/shard_map/solve/pallas_call | solution.py:417
where the time goes:
time: 44.6 us; the launch traced here: 44.5 us
  Pallas kernels  43.9 us (98%)
  between operations  0.64 us (1%)
    pallas_call x1, Pallas kernels, body(): pl.pallas_call(exchange_kernel, out_shape=(jax.ShapeDtypeStruct((NF, K, K...  41.4 us
    pallas_call x1, Pallas kernels, body(): pl.pallas_call(solve_kernel, out_shape=(jax.ShapeDtypeStruct((NF, 32, LB)...  2.47 us

commit v1 on v0

--- a/solution.py
+++ b/solution.py
@@ -100,6 +100,12 @@
 
     partner = (fr, z * 2 + (1 - core), gc)
 
+    barrier = pltpu.get_barrier_semaphore()
+    for d in range(1, 16):
+        pl.semaphore_signal(barrier, inc=1, device_id=g_peer(d)[1], device_id_type=MESH)
+    for d in PEERS:
+        pl.semaphore_signal(barrier, inc=1, device_id=c_peer(d)[1], device_id_type=MESH)
+
     loads = []
     own_child = []
     for f in range(NF):
@@ -117,11 +123,6 @@
     picks_load = pltpu.make_async_copy(picks_hbm, picks_ref, load_sem.at[10])
     picks_load.start()
 
-    barrier = pltpu.get_barrier_semaphore()
-    for d in range(1, 16):
-        pl.semaphore_signal(barrier, inc=1, device_id=g_peer(d)[1], device_id_type=MESH)
-    for d in PEERS:
-        pl.semaphore_signal(barrier, inc=1, device_id=c_peer(d)[1], device_id_type=MESH)
     own_map.wait()
     lane = lax.broadcasted_iota(I32, (1, 128), 1)
     tile = []
@@ -244,17 +245,17 @@
         if f == NF - 1:
             en1[gr] = jnp.concatenate(energies + [jnp.zeros((8 - NF, 128), F32)], axis=0)
             for d in range(1, 16):
-                send(en1.at[gr], en1.at[gr], e1_s.at[d - 1], e1_r.at[gr], g_peer(d)[1])
+                send(en1.at[gr, 0:NF, :], en1.at[gr, 0:NF, :], e1_s.at[d - 1], e1_r.at[gr], g_peer(d)[1])
         for slot, d in enumerate(PEERS):
             cc, device = c_peer(d)
             send(ag_in.at[f, gc, 0:MSG, :], ag_in.at[f, gc, 0:MSG, :], ag_s.at[f, slot], ag_r.at[f, gc], device)
 
     for d in range(1, 16):
         gg, device = g_peer(-d)
-        arrive(en1.at[gg], e1_s.at[d - 1], e1_r.at[gg], device)
+        arrive(en1.at[gg, 0:NF, :], e1_s.at[d - 1], e1_r.at[gg], device)
     en2[gc] = functools.reduce(lambda a, b: a + b, [en1[g] for g in range(16)])
     for slot, d in enumerate(PEERS):
-        send(en2.at[gc], en2.at[gc], e2_s.at[slot], e2_r.at[gc], c_peer(d)[1])
+        send(en2.at[gc, 0:NF, :], en2.at[gc, 0:NF, :], e2_s.at[slot], e2_r.at[gc], c_peer(d)[1])
 
     for f in range(NF):
         if f == NF - 1:
@@ -290,7 +291,7 @@
 
     for d in PEERS:
         cc, device = c_peer(d)
-        arrive(en2.at[cc], e2_s.at[0], e2_r.at[cc], device)
+        arrive(en2.at[cc, 0:NF, :], e2_s.at[0], e2_r.at[cc], device)
     energy_ref[...] = functools.reduce(lambda a, b: a + b, [en2[c] for c in range(NC)])
 
 

time: 44.6 us -> 44.5 us (level)
  no operation moved by 1% of the time
where the time goes in v1:
time: 44.5 us; the launch traced here: 44.4 us
  Pallas kernels  43.8 us (98%)
  between operations  0.64 us (1%)
    pallas_call x1, Pallas kernels, body(): pl.pallas_call(exchange_kernel, out_shape=(jax.ShapeDtypeStruct((NF, K, K...  41.3 us
    pallas_call x1, Pallas kernels, body(): pl.pallas_call(solve_kernel, out_shape=(jax.ShapeDtypeStruct((NF, 32, LB)...  2.47 us

profile of v1, /device:TPU:1, one launch (start us, length us, event | category | flops | bytes accessed | tf_op | source)
XLA Modules:
  0.0 44.4 jit_solution(7165890019285689125)
XLA Ops:
  0.6 41.3 %exchange.1 = (f32[3,128,128]{2,1,0:T(8,128)S(1)}, f32[3,512,128]{2,1,0:T(8,128)S(1)}, f32[3,32,512]{2,1,0:T(8,128)S(1)}, f32[8,128]{1,0:T(8,128)S(1)}, bf16[3,128,256]{2,1,0:T(8,128)(2,1)S(1)}) custom-call(bf16[3,512,1024]{2,1,0:T(8,128)(2,1)} %front_hbm.1, bf16[3,1024,256]{2,1,0:T(8,128)(2,1)} %omega_hbm.1, bf16[3,32,256]{2,1,0:T(8,128)(2,1)} %bitcast.2, ...), custom_call_target="tpu_custom_call" | custom-call | tf_op jit(solution)/shard_map/exchange/pallas_call | solution.py:376
  41.9 2.5 %solve.1 = (f32[3,32,512]{2,1,0:T(8,128)}, f32[3,512,128]{2,1,0:T(8,128)}, bf16[3,128,256]{2,1,0:T(8,128)(2,1)}) custom-call(f32[3,128,128]{2,1,0:T(8,128)S(1)} %get-tuple-element.11.gram_ref, f32[3,512,128]{2,1,0:T(8,128)S(1)} %get-tuple-element.12.cross_ref, f32[3,32,512]{2,1,0:T(8,128)S(1)} %get-tuple-element.13.own_ref, ...), custom_call_target="tpu_custom_call" | custom-call | tf_op jit(solution)/shard_map/solve/pallas_call | solution.py:418
